TPU v7x, 32 devices: a whole 2x2x4 slice. The times are simulated.
32 devices in a mesh: req: 16 (over z, y, x), head: 2 (over core).
Axes of the slice: x: 2, y: 2, z: 4, core: 2. Of those that a mesh axis runs over, the one named last changes fastest.
Arguments:
- tokens: bfloat16 [80, 1024], P('req'), may hold values from -6 to 6
- norm_gain: float32 [1024], replicated, may hold values from 0.1 to 1.9
- w_qkv: bfloat16 [1024, 8, 384], P(None, 'head'), may hold values from -0.1875 to 0.1875
- persist_kv: bfloat16 [8, 16, 256], P('head'), may hold values from -9 to 9
- memory: bfloat16 [16, 8, 128, 128], P('req', 'head'), may hold values from -0.5 to 0.5
- cache_kv: bfloat16 [128, 512, 8, 256], P('req', None, 'head')
- piece_owner: int32 [128], P('req'), may hold values from 0 to 15, as said below
- piece_len: int32 [128], P('req'), may hold values from 1 to 512, as said below
- w_out: bfloat16 [8, 128, 1024], P('head'), may hold values from -0.1875 to 0.1875
Outputs:
- layer_out: bfloat16 [80, 1024], P('req', 'head')
Inputs may be any that keep to these rules, and one draw needn't show every extreme that they name: `piece_owner`: every request owns 1 to 16 pieces, and one request owns exactly 16. `piece_len`: some piece is full.
All inputs are finite; a program needn't handle non-finite values.
Results may differ from a plain program's by a relative error of at most 0.009.
The roundings to bfloat16 on the way count: a program that leaves them out, or rounds other values in their place, can miss the bound.
Values may be sent and summed in bfloat16 or wider, within the bound.
A program may use at most 64 MiB of HBM per device.

v0:
```python
import jax
import jax.numpy as jnp
from jax import lax
from jax.sharding import PartitionSpec as P

DH = 128
NP = 16
Q = 5
PIECE = 512


masked_score = -1e30
norm_eps = 1e-06


def merged(shard, axis, combine):
    everything = jax.tree.map(lambda part: lax.all_gather(part, axis), shard)
    leading = jax.tree.map(lambda part: part[0], everything)

    def step(k, so_far):
        return combine(so_far, jax.tree.map(lambda part: part[k], everything))

    return lax.fori_loop(1, lax.axis_size(axis), step, leading)


def join_parts(first, second):
    peak = jnp.maximum(first[0], second[0])
    scale_one = jnp.exp(first[0] - peak)
    scale_two = jnp.exp(second[0] - peak)
    total = first[1] * scale_one + second[1] * scale_two
    summed = first[2] * scale_one[..., None] + second[2] * scale_two[..., None]
    return (peak, total, summed)


def dense_parts(peaks, totals, summed, piece_owner, total_reqs):
    f32 = jnp.float32
    onehot = piece_owner[:, None] == jnp.arange(total_reqs, dtype=jnp.int32)[None, :]
    peak_dev = jnp.max(jnp.where(onehot[:, :, None, None], peaks[:, None], masked_score), axis=0)
    factor = jnp.exp(peaks - peak_dev[piece_owner])
    onehot_f = onehot.astype(f32)
    total_dev = jnp.einsum(
        "sr,shq->rhq", onehot_f, totals * factor, precision=lax.Precision.HIGHEST
    )
    summed_dev = jnp.einsum(
        "sr,shqe->rhqe", onehot_f, summed * factor[..., None], precision=lax.Precision.HIGHEST
    )
    return (peak_dev, total_dev, summed_dev)


def shards(tokens, norm_gain, w_qkv, persist_kv, memory, cache_kv, piece_owner, piece_len, w_out):
    f32 = jnp.float32
    rows = tokens.shape[0]
    heads = w_qkv.shape[1]
    req_dev = memory.shape[0]
    xf = tokens.astype(f32)
    normed = (
        xf * lax.rsqrt(jnp.mean(xf * xf, axis=-1, keepdims=True) + norm_eps) * norm_gain
    ).astype(jnp.bfloat16)
    proj = jnp.einsum("td,dhe->the", normed, w_qkv, preferred_element_type=f32)
    query = (proj[..., :DH] * DH ** (-0.5)).astype(jnp.bfloat16)
    new_key = proj[..., DH : 2 * DH].astype(jnp.bfloat16)
    new_value = proj[..., 2 * DH :].astype(jnp.bfloat16)
    all_query = lax.all_gather(query, "req", axis=0, tiled=True)
    query_all4 = all_query.reshape(-1, Q, heads, DH)
    total_reqs = query_all4.shape[0]
    query_rows = query_all4[piece_owner]
    scores = jnp.einsum(
        "sqhe,skhe->shqk", query_rows, cache_kv[..., :DH], preferred_element_type=f32
    )
    valid = (jnp.arange(PIECE)[None, :] < piece_len[:, None])[:, None, None, :]
    scores = jnp.where(valid, scores, masked_score)
    peaks = jnp.max(scores, axis=-1)
    weight = jnp.where(valid, jnp.exp(scores - peaks[..., None]), 0.0)
    totals = jnp.sum(weight, axis=-1)
    summed = jnp.einsum(
        "shqk,skhe->shqe",
        weight.astype(jnp.bfloat16),
        cache_kv[..., DH:],
        preferred_element_type=f32,
    )
    peak_dev, total_dev, summed_dev = dense_parts(peaks, totals, summed, piece_owner, total_reqs)
    peak_all, total_all, summed_all = merged((peak_dev, total_dev, summed_dev), "req", join_parts)
    start = lax.axis_index("req") * req_dev
    peak_cache = lax.dynamic_slice_in_dim(peak_all, start, req_dev, 0)
    total_cache = lax.dynamic_slice_in_dim(total_all, start, req_dev, 0)
    summed_cache = lax.dynamic_slice_in_dim(summed_all, start, req_dev, 0)
    query4 = query.reshape(req_dev, Q, heads, DH)
    key4 = new_key.reshape(req_dev, Q, heads, DH)
    value4 = new_value.reshape(req_dev, Q, heads, DH)
    score_persist = jnp.einsum(
        "rqhe,hne->rhqn", query4, persist_kv[..., :DH], preferred_element_type=f32
    )
    score_new = jnp.einsum("rqhe,rkhe->rhqk", query4, key4, preferred_element_type=f32)
    causal = jnp.arange(Q)[:, None] >= jnp.arange(Q)[None, :]
    score_new = jnp.where(causal, score_new, masked_score)
    score_own = jnp.concatenate([score_persist, score_new], axis=-1)
    peak_own = jnp.max(score_own, axis=-1)
    weight_own = jnp.exp(score_own - peak_own[..., None])
    total_own = jnp.sum(weight_own, axis=-1)
    rounded_own = weight_own.astype(jnp.bfloat16)
    summed_own = jnp.einsum(
        "rhqn,hne->rhqe", rounded_own[..., :NP], persist_kv[..., DH:], preferred_element_type=f32
    )
    summed_own = summed_own + jnp.einsum(
        "rhqk,rkhe->rhqe", rounded_own[..., NP:], value4, preferred_element_type=f32
    )
    peak_total = jnp.maximum(peak_cache, peak_own)
    scale_cache = jnp.exp(peak_cache - peak_total)
    scale_own = jnp.exp(peak_own - peak_total)
    total_final = total_cache * scale_cache + total_own * scale_own
    summed_final = summed_cache * scale_cache[..., None] + summed_own * scale_own[..., None]
    attended = summed_final / total_final[..., None]
    recalled = jnp.einsum("rqhe,rhef->rhqf", query4, memory, preferred_element_type=f32)
    head_out = (attended + recalled).astype(jnp.bfloat16)
    head_out = jnp.transpose(head_out, (0, 2, 1, 3)).reshape(rows, heads, DH)
    partial_out = jnp.einsum("thd,hdf->tf", head_out, w_out, preferred_element_type=f32)
    return lax.psum_scatter(partial_out, "head", scatter_dimension=1, tiled=True).astype(
        jnp.bfloat16
    )


def solution(mesh):
    in_specs = (
        P("req", None),
        P(),
        P(None, "head", None),
        P("head", None, None),
        P("req", "head", None, None),
        P("req", None, "head", None),
        P("req"),
        P("req"),
        P("head", None, None),
    )
    out_specs = P("req", "head")
    return jax.shard_map(shards, mesh=mesh, in_specs=in_specs, out_specs=out_specs, check_vma=False)
```

profile of v0, /device:TPU:0, one launch (start us, length us, event | category | flops | bytes accessed | tf_op | source)
XLA Modules:
  0.0 213.4 jit_solution(4292865089126093993)
XLA Ops:
  6.5 0.8 compare_select_fusion
  7.3 0.9 iota_compare_fusion.2
  8.2 0.8 fusion.34
  9.1 1.3 fusion.66
  10.4 42.8 %all_gather.21 = bf16[80,4,128]{2,1,0:T(4,128)(2,1)S(1)} all-gather(bf16[5,4,128]{2,1,0:T(4,128)(2,1)S(1)} %copy.77), channel_id=1, replica_groups=mesh['req'=16,'head'=2] {'req'}, dimensions={0}, use_global_device_ids=true | all-gather | bytes 87040 | tf_op jit(solution)/shard_map/all_gather | solution.py:63
  53.2 0.7 iota_compare_fusion
  53.9 8.1 %fusion.65 = (bf16[8,512,4,128]{3,2,1,0:T(4,128)(2,1)}, bf16[8,512,4,128]{3,2,1,0:T(4,128)(2,1)}) fusion(bf16[8,512,4,256]{3,2,1,0:T(4,128)(2,1)} %param.16), kind=kLoop, calls=%fused_computation.88 | loop fusion | bytes 16777216 | tf_op jit(solution)/shard_map/slice | solution.py:78
  62.0 0.6 gather_fusion
  62.6 4.2 %fusion.67 = (f32[8,4,5]{2,1,0:T(4,128)S(1)}, f32[8,4,5,512]{3,2,1,0:T(8,128)}) fusion(bf16[8,512,4,128]{3,2,1,0:T(4,128)(2,1)} %get-tuple-element.237, bf16[8,5,4,128]{3,2,1,0:T(4,128)(2,1)S(1)} %gather_fusion, pred[8,512]{1,0:T(8,128)(4,1)S(1)} %iota_compare_fusion), kind=kOutput, calls=%fused_computation.90 | convolution fusion | flops 21135200 | bytes 4567680 | tf_op jit(solution)/shard_map/sqhe,skhe->shqk/dot_general | solution.py:67
  66.9 1.3 fusion.24
  68.5 0.6 gather_fusion.1
  69.1 3.1 %fusion.13 = f32[8,4,5,128]{3,2,1,0:T(8,128)S(1)} fusion(bf16[8,512,4,128]{3,2,1,0:T(4,128)(2,1)} %get-tuple-element.236, f32[8,4,5,512]{3,2,1,0:T(8,128)} %get-tuple-element.245, f32[8,4,5]{2,1,0:T(4,128)S(1)} %get-tuple-element.244, pred[8,512]{1,0:T(8,128)(4,1)S(1)} %iota_compare_fusion, f32[8,4,5]{2,1,0:T(4,128)S(1)} %bitcast.126), kind=kOutput, calls=%fused_computation.19 | convolution fusion | flops 21237760 | bytes 4609280 | tf_op jit(solution)/shard_map/shqk,skhe->shqe/dot_general | solution.py:75
  72.2 1.0 fusion.31
  73.6 40.2 %all-gather.1 = f32[256,4,5]{2,1,0:T(4,128)S(1)} all-gather(f32[16,4,5]{2,1,0:T(4,128)S(1)} %copy.84), channel_id=3, replica_groups=mesh['req'=16,'head'=2] {'req'}, dimensions={0}, use_global_device_ids=true | all-gather | bytes 21760 | tf_op jit(solution)/shard_map/all_gather | solution.py:17
  113.7 0.8 copy-done.1
  114.5 2.2 %copy.93 = f32[16,16,4,5]{1,2,3,0:T(4,128)} copy(f32[16,16,4,5]{3,2,1,0:T(4,128)} %bitcast.116) | data formatting | bytes 40960 | tf_op jit(solution)/shard_map/while | solution.py:23
  116.8 42.2 %all-gather = f32[256,4,5]{2,1,0:T(4,128)S(1)} all-gather(f32[16,4,5]{2,1,0:T(4,128)S(1)} %copy.81), channel_id=2, replica_groups=mesh['req'=16,'head'=2] {'req'}, dimensions={0}, use_global_device_ids=true | all-gather | bytes 21760 | tf_op jit(solution)/shard_map/all_gather | solution.py:17
  159.0 0.8 copy-done.2
  159.8 2.2 %copy.92 = f32[16,16,4,5]{1,2,3,0:T(4,128)} copy(f32[16,16,4,5]{3,2,1,0:T(4,128)} %bitcast.117) | data formatting | bytes 40960 | tf_op jit(solution)/shard_map/while | solution.py:23
  162.1 0.7 fusion.69
  162.8 0.7 fusion.68
  163.6 0.9 slice.60
  164.6 32.8 %while.19 = (s32[]{:T(128)}, f32[16,4,5]{0,1,2:T(4,128)S(1)}, f32[16,4,5]{0,1,2:T(4,128)S(1)}, f32[16,4,5,128]{3,2,1,0:T(8,128)S(1)}, f32[16,16,4,5]{1,2,3,0:T(4...) while((s32[]{:T(128)}, f32[16,4,5]{0,1,2:T(4,128)S(1)}, ...), condition=%wide.region_5.6_spmd, body=%wide.region_4.5_spmd.sunk | while | flops 124805 | bytes 837271 | solution.py:23
  164.6 0.8 fusion.76
  165.6 0.9 constant_dynamic-slice_fusion.2
  166.8 0.8 fusion.76
  167.7 0.9 constant_dynamic-slice_fusion.2
  169.0 0.8 fusion.76
  169.9 0.9 constant_dynamic-slice_fusion.2
  170.9 0.3 fusion.77
  171.1 0.8 fusion.76
  172.1 0.9 constant_dynamic-slice_fusion.2
  173.0 0.3 fusion.77
  173.3 0.8 fusion.76
  174.3 0.9 constant_dynamic-slice_fusion.2
  175.5 0.8 fusion.76
  176.5 0.9 constant_dynamic-slice_fusion.2
  177.7 0.8 fusion.76
  178.7 0.9 constant_dynamic-slice_fusion.2
  179.6 0.3 fusion.77
  179.9 0.8 fusion.76
  180.8 0.9 constant_dynamic-slice_fusion.2
  181.8 0.3 fusion.77
  182.1 0.8 fusion.76
  183.0 0.9 constant_dynamic-slice_fusion.2
  184.0 0.3 fusion.77
  184.3 0.8 fusion.76
  185.2 0.9 constant_dynamic-slice_fusion.2
  186.1 0.3 fusion.77
  186.4 0.8 fusion.76
  187.4 0.9 constant_dynamic-slice_fusion.2
  188.6 0.8 fusion.76
  189.6 0.9 constant_dynamic-slice_fusion.2
  190.8 0.8 fusion.76
  191.8 0.9 constant_dynamic-slice_fusion.2
  193.0 0.8 fusion.76
  194.0 0.9 constant_dynamic-slice_fusion.2
  195.2 0.8 fusion.76
  196.1 0.9 constant_dynamic-slice_fusion.2
  197.6 0.9 fusion.52
  198.7 0.8 fusion.20
  199.5 2.3 %convolution_bitcast_fusion = f32[5,1024]{1,0:T(8,128)} fusion(bf16[4,128,1024]{2,1,0:T(8,128)(2,1)} %param.19, f32[1,4,5,128]{3,2,1,0:T(8,128)S(1)} %fusion.20, bf16[5,4,128]{2,0,1:T(8,128)(2,1)S(1)} %fusion.39, bf16[1,4,128,128]{3,2,1,0:T(8,128)(2,1)} %param.15), kind=kOutput, calls=%fused_computation.20 | convolution fusion | flops 5903360 | bytes 1215488 | tf_op jit(solution)/shard_map/thd,hdf->tf/dot_general | solution.py:116
  201.8 3.4 %reduce-scatter.2.cloned.1.call-done = f32[5,512]{1,0:T(8,128)} async-done(((f32[5,1024]{1,0:T(8,128)}), f32[5,512]{1,0:T(8,128)}) %reduce-scatter.2.cloned.1.call-update) | async-done | bytes 10256 | tf_op jit(solution)/shard_map/reduce_scatter | solution.py:117
  205.3 1.3 convert_element_type.38
  (73 shorter events, 7.0 us)
Async XLA Ops:
  6.5 2.5 %copy-start = (bf16[1024,4,384]{2,1,0:T(4,128)(2,1)S(1)}, bf16[1024,4,384]{2,1,0:T(4,128)(2,1)}, u32[]{:S(2)}) copy-start(bf16[1024,4,384]{2,1,0:T(4,128)(2,1)} %param.13) | copy-start | bytes 9437188
  6.5 157.0 %all-gather.5.cloned.1.call-start = ((), (), s32[]{:S(2)}) async-start(), calls=%async_computation.2 | async-start | bytes 2785280 | tf_op jit(solution)/shard_map/all_gather | solution.py:17
  62.6 9.6 %copy-start.4 = (s32[8]{0:T(128)S(1)}, s32[8]{0:T(128)}, u32[]{:S(2)}) copy-start(s32[8]{0:T(128)} %param.17) | copy-start | bytes 100
  69.0 93.8 %copy-start.3 = (bf16[4,16,256]{2,1,0:T(8,128)(2,1)S(1)}, bf16[4,16,256]{2,1,0:T(8,128)(2,1)}, u32[]{:S(2)}) copy-start(bf16[4,16,256]{2,1,0:T(8,128)(2,1)} %param.14) | copy-start | bytes 98308
  73.2 132.1 %reduce-scatter.2.cloned.1.call-start = ((), (), s32[]{:S(2)}) async-start(), calls=%async_computation.1 | async-start | bytes 49152 | tf_op jit(solution)/shard_map/reduce_scatter | solution.py:117
  113.7 0.8 copy-start.1
  159.0 0.8 copy-start.2
Sparse Core Ops, SparseCore 0:
  73.3 67.9 all-gather.4
  201.9 3.2 reduce-scatter.1
where the time goes:
time: 216 us; the launch traced here: 213 us
  blocking collectives  125 us (58%)
  local copies, waits for them, and re-layouts  34.1 us (16%)
  other arithmetic  22.1 us (10%)
  matrix products  14.6 us (7%)
  between operations  13.5 us (6%)
  waiting for transfers between devices  3.48 us (2%)
    all_gather x2, blocking collectives, merged(): everything = jax.tree.map(lambda part: lax.all_gather(part, axis), shard)  82.4 us
    all_gather x1, blocking collectives, shards(): all_query = lax.all_gather(query, 'req', axis=0, tiled=True)  42.8 us
    dynamic_slice x15, local copies, waits for them, and re-layouts, step(): return combine(so_far, jax.tree.map(lambda part: part[k], everything))  13.9 us
    add x15, other arithmetic, join_parts(): total = first[1] * scale_one + second[1] * scale_two  11.3 us
    slice x1, local copies, waits for them, and re-layouts, shards(): cache_kv[..., DH:]  8.08 us
    while x7, local copies, waits for them, and re-layouts, merged(): return lax.fori_loop(1, lax.axis_size(axis), step, leading)  4.8 us
  transfers between devices with their start and end apart: 2, of which 1 were waited for; matrix products, arithmetic and copies ran while one was open for 3% of the time, Pallas kernels for 0%

commit v1 on v0

v1 whole, which is shorter than its diff:
```python
import functools

import jax
import jax.numpy as jnp
from jax import lax
from jax.experimental import pallas as pl
from jax.experimental.pallas import tpu as pltpu
from jax.sharding import PartitionSpec as P

DH = 128
NP = 16
Q = 5
MESH = pl.DeviceIdType.MESH

masked_score = -1e30
norm_eps = 1e-06
f32 = jnp.float32
bf16 = jnp.bfloat16


def dot(a, b):
    return jnp.dot(a, b, preferred_element_type=f32)


def dot_t(a, b):
    return lax.dot_general(a, b, (((1,), (1,)), ((), ())), preferred_element_type=f32)


def iota(shape, dim):
    return lax.broadcasted_iota(jnp.int32, shape, dim)


def three_terms(x):
    high = x.astype(bf16).astype(f32)
    middle = (x - high).astype(bf16).astype(f32)
    return [high, middle, x - high - middle]


def kernel(
    n, nh, heads, pieces, rows_f, rows,
    qkv_ref, persist_ref, owner_ref, len_ref, cache_ref, memory_ref, w_out_ref,
    out_ref,
    keys, values, memory, w_out, all_query, outbox, inbox, partial, halves,
    key_sem, value_sem, weight_sem, q_send, q_recv, p_send, p_recv, h_send, h_recv,
):
    me = lax.axis_index("req")
    my_head = lax.axis_index("head")
    columns = partial.shape[-1]
    slots = cache_ref.shape[1]

    def cache_copies(s):
        if heads > 1:
            key_view, value_view = cache_ref.at[s, :, 0], cache_ref.at[s, :, 1]
        else:
            key_view, value_view = cache_ref.at[s, :, pl.ds(0, DH)], cache_ref.at[s, :, pl.ds(DH, DH)]
        return (
            pltpu.make_async_copy(key_view, keys.at[s], key_sem.at[s]),
            pltpu.make_async_copy(value_view, values.at[s], value_sem.at[s]),
        )

    memory_copy = pltpu.make_async_copy(memory_ref, memory, weight_sem.at[0])
    w_out_copy = pltpu.make_async_copy(w_out_ref, w_out, weight_sem.at[1])
    memory_copy.start()
    for s in range(pieces):
        for copy in cache_copies(s):
            copy.start()
    w_out_copy.start()

    barrier = pltpu.get_barrier_semaphore()

    @pl.loop(1, n)
    def _(k):
        pl.semaphore_signal(barrier, inc=1, device_id={"req": lax.rem(me + k, n)}, device_id_type=MESH)

    @pl.loop(1, nh)
    def _(k):
        pl.semaphore_signal(barrier, inc=1, device_id={"head": lax.rem(my_head + k, nh)}, device_id_type=MESH)

    all_query[me] = qkv_ref[:, :DH]
    pl.semaphore_wait(barrier, n - 1 + nh - 1)

    def query_copy(slot, other):
        return pltpu.make_async_remote_copy(
            src_ref=all_query.at[slot], dst_ref=all_query.at[slot],
            send_sem=q_send.at[other], recv_sem=q_recv.at[slot],
            device_id={"req": other}, device_id_type=MESH,
        )

    @pl.loop(1, n)
    def _(k):
        query_copy(me, lax.rem(me + k, n)).start()

    query = qkv_ref[:, :DH]
    query_f = query[:rows_f]
    persist = persist_ref[...]
    row = iota((rows_f, 1), 0)
    row_head, row_token = row % heads, row // heads
    col = iota((1, heads * NP), 1)
    score_persist = jnp.where(row_head == col // NP, dot_t(query_f, persist[:, :DH]), masked_score)
    col = iota((1, rows), 1)
    seen = (row_head == col % heads) & (col // heads <= row_token) & (col < Q * heads)
    score_new = jnp.where(seen, dot_t(query_f, qkv_ref[:, DH : 2 * DH]), masked_score)
    m_own = jnp.maximum(
        jnp.max(score_persist, axis=-1, keepdims=True), jnp.max(score_new, axis=-1, keepdims=True)
    )
    w_persist = jnp.exp(score_persist - m_own)
    w_new = jnp.exp(score_new - m_own)
    l_own = jnp.sum(w_persist, axis=-1, keepdims=True) + jnp.sum(w_new, axis=-1, keepdims=True)
    o_own = dot(w_persist.astype(bf16), persist[:, DH:]) + dot(w_new.astype(bf16), qkv_ref[:, 2 * DH :])
    memory_copy.wait()
    recalled = jnp.zeros((rows_f, DH), f32)
    for h in range(heads):
        recalled = jnp.where(row_head == h, dot(query_f, memory[h]), recalled)

    @pl.loop(1, n)
    def _(k):
        query_copy(lax.rem(me + k, n), lax.rem(me + k, n)).wait_recv()

    col = iota((1, slots * heads), 1)
    same_head = row_head == col % heads
    col_slot = col // heads
    key_rows = keys.reshape(pieces, slots * heads, DH)
    value_rows = values.reshape(pieces, slots * heads, DH)
    owners, peaks, totals, sums = [], [], [], []
    for s in range(pieces):
        owner = owner_ref[s]
        key_copy, value_copy = cache_copies(s)
        key_copy.wait()
        valid = same_head & (col_slot < len_ref[s])
        scores = jnp.where(valid, dot_t(all_query[owner][:rows_f], key_rows[s]), masked_score)
        peak = jnp.max(scores, axis=-1, keepdims=True)
        weight = jnp.where(valid, jnp.exp(scores - peak), 0.0)
        value_copy.wait()
        owners.append(owner)
        peaks.append(peak)
        totals.append(jnp.sum(weight, axis=-1, keepdims=True))
        sums.append(dot(weight.astype(bf16), value_rows[s]))

    shared = []
    for s in range(pieces):
        peak = peaks[s]
        for other in range(pieces):
            if other != s:
                peak = jnp.maximum(peak, jnp.where(owners[other] == owners[s], peaks[other], masked_score))
        shared.append(peak)
    for s in range(pieces):
        factor = jnp.exp(peaks[s] - shared[s])
        totals[s] = totals[s] * factor
        sums[s] = sums[s] * factor

    eye = iota((rows_f, DH), 0) == iota((rows_f, DH), 1)
    zeros_tail = jnp.zeros((2, DH), f32)

    def as_row(column):
        return jnp.sum(jnp.where(eye, column, 0.0), axis=0, keepdims=True)

    def message(r):
        m = jnp.full((rows_f, 1), masked_score, f32)
        l = jnp.zeros((rows_f, 1), f32)
        o = jnp.zeros((rows_f, DH), f32)
        for s in range(pieces):
            mine = owners[s] == r
            m = jnp.where(mine, shared[s], m)
            l = l + jnp.where(mine, totals[s], 0.0)
            o = o + jnp.where(mine, sums[s], 0.0)
        tail = three_terms(as_row(m)) + three_terms(as_row(l)) + [zeros_tail]
        return jnp.concatenate([o] + tail, axis=0).astype(bf16)

    def partial_copy(mine, other):
        return pltpu.make_async_remote_copy(
            src_ref=outbox.at[other], dst_ref=inbox.at[mine],
            send_sem=p_send.at[other], recv_sem=p_recv.at[mine],
            device_id={"req": other}, device_id_type=MESH,
        )

    @pl.loop(1, n)
    def _(k):
        other = lax.rem(me + k, n)
        outbox[other] = message(other)
        partial_copy(me, other).start()

    inbox[me] = message(me)

    @pl.loop(1, n)
    def _(k):
        other = lax.rem(me + k, n)
        partial_copy(other, other).wait_recv()

    got = inbox[...].astype(f32)
    tail = got[:, rows_f:]
    m_all = tail[:, 0:1] + (tail[:, 1:2] + tail[:, 2:3])
    l_all = tail[:, 3:4] + (tail[:, 4:5] + tail[:, 5:6])
    m_cache = jnp.max(m_all, axis=0)
    factor = jnp.exp(m_all - m_cache[None])
    l_cache = jnp.sum(l_all * factor, axis=0)

    def as_column(rows_):
        return jnp.sum(jnp.where(eye, rows_, 0.0), axis=-1, keepdims=True)

    o_cache = jnp.zeros((rows_f, DH), f32)
    for k in range(n):
        o_cache = o_cache + got[k, :rows_f] * as_column(factor[k])
    m_cache, l_cache = as_column(m_cache), as_column(l_cache)
    m = jnp.maximum(m_cache, m_own)
    scale_cache, scale_own = jnp.exp(m_cache - m), jnp.exp(m_own - m)
    total = l_cache * scale_cache + l_own * scale_own
    attended = (o_cache * scale_cache + o_own * scale_own) / total
    head_out = (attended + recalled).astype(bf16)

    target, source = iota((8 * heads, rows_f), 0), iota((8 * heads, rows_f), 1)
    pick = (target % 8 < Q) & (source == (target % 8) * heads + target // 8)
    by_head = dot(pick.astype(f32).astype(bf16), head_out)
    lanes = jnp.concatenate([by_head[8 * h : 8 * h + 8] for h in range(heads)], axis=1).astype(bf16)
    w_out_copy.wait()
    layer = dot(lanes, w_out[...].reshape(heads * DH, nh * columns))
    for k in range(nh):
        partial[k] = layer[:, k * columns : (k + 1) * columns]

    def half_copy(mine, other):
        return pltpu.make_async_remote_copy(
            src_ref=partial.at[other], dst_ref=halves.at[mine],
            send_sem=h_send.at[other], recv_sem=h_recv.at[mine],
            device_id={"head": other}, device_id_type=MESH,
        )

    @pl.loop(1, nh)
    def _(k):
        half_copy(my_head, lax.rem(my_head + k, nh)).start()

    halves[my_head] = partial[my_head]

    @pl.loop(1, nh)
    def _(k):
        other = lax.rem(my_head + k, nh)
        half_copy(other, other).wait_recv()

    out_ref[...] = jnp.sum(halves[...], axis=0)[:Q].astype(bf16)

    @pl.loop(1, n)
    def _(k):
        other = lax.rem(me + k, n)
        query_copy(me, other).wait_send()
        partial_copy(me, other).wait_send()

    @pl.loop(1, nh)
    def _(k):
        half_copy(my_head, lax.rem(my_head + k, nh)).wait_send()


def shards(n, nh, tokens, norm_gain, w_qkv, persist_kv, memory, cache_kv, piece_owner, piece_len, w_out):
    heads = w_qkv.shape[1]
    pieces, slots = cache_kv.shape[:2]
    columns = w_out.shape[2] // nh
    rows_f = -(-(Q * heads - 8) // 16) * 16 + 8
    rows = rows_f + 8
    xf = tokens.astype(f32)
    normed = (
        xf * lax.rsqrt(jnp.mean(xf * xf, axis=-1, keepdims=True) + norm_eps) * norm_gain
    ).astype(bf16)
    proj = jnp.einsum("td,dhe->the", normed, w_qkv, preferred_element_type=f32)
    scale = jnp.where(jnp.arange(3 * DH) < DH, DH ** (-0.5), 1.0)
    qkv = (proj * scale).astype(bf16).reshape(Q * heads, 3 * DH)
    qkv = jnp.pad(qkv, ((0, rows - Q * heads), (0, 0)))
    if heads > 1:
        cache = cache_kv.reshape(pieces, slots, heads, 2, DH).transpose(0, 1, 3, 2, 4)
        cache_shape = (pieces, slots, heads, DH)
    else:
        cache = cache_kv.reshape(pieces, slots, 2 * DH)
        cache_shape = (pieces, slots, DH)
    vmem = pl.BlockSpec(memory_space=pltpu.VMEM)
    smem = pl.BlockSpec(memory_space=pltpu.SMEM)
    hbm = pl.BlockSpec(memory_space=pl.ANY)
    dma = pltpu.SemaphoreType.DMA
    return pl.pallas_call(
        functools.partial(kernel, n, nh, heads, pieces, rows_f, rows),
        out_shape=jax.ShapeDtypeStruct((Q, columns), bf16),
        in_specs=[vmem, vmem, smem, smem, hbm, hbm, hbm],
        out_specs=vmem,
        scratch_shapes=[
            pltpu.VMEM(cache_shape, bf16),
            pltpu.VMEM(cache_shape, bf16),
            pltpu.VMEM((heads, DH, DH), bf16),
            pltpu.VMEM((heads, DH, nh * columns), bf16),
            pltpu.VMEM((n, rows, DH), bf16),
            pltpu.VMEM((n, rows, DH), bf16),
            pltpu.VMEM((n, rows, DH), bf16),
            pltpu.VMEM((nh, 8, columns), f32),
            pltpu.VMEM((nh, 8, columns), f32),
            dma((pieces,)), dma((pieces,)), dma((2,)),
            dma((n,)), dma((n,)), dma((n,)), dma((n,)), dma((nh,)), dma((nh,)),
        ],
        compiler_params=pltpu.CompilerParams(
            collective_id=0, has_side_effects=True, vmem_limit_bytes=48 * 2**20
        ),
        cost_estimate=pl.CostEstimate(flops=100_000_000, bytes_accessed=10_000_000, transcendentals=500_000),
    )(
        qkv, persist_kv.reshape(heads * NP, 2 * DH), piece_owner, piece_len, cache,
        memory.reshape(heads, DH, DH), w_out,
    )


def solution(mesh):
    in_specs = (
        P("req", None),
        P(),
        P(None, "head", None),
        P("head", None, None),
        P("req", "head", None, None),
        P("req", None, "head", None),
        P("req"),
        P("req"),
        P("head", None, None),
    )
    n, nh = mesh.shape["req"], mesh.shape["head"]
    return jax.shard_map(
        functools.partial(shards, n, nh), mesh=mesh, in_specs=in_specs, out_specs=P("req", "head"), check_vma=False
    )
```

time: 216 us -> 30.7 us (0.14)
  blocking collectives: 125 us -> 0 us
  local copies, waits for them, and re-layouts: 34.1 us -> 2.76 us
  Pallas kernels: 0 us -> 25.2 us
  other arithmetic: 22.1 us -> 1 us
  between operations: 13.5 us -> 0.08 us
  matrix products: 14.6 us -> 1.27 us
  waiting for transfers between devices: 3.48 us -> 0 us
    all_gather x3 -> x0, blocking collectives: 125 us -> none  [the longest x2 82.4 us: merged(): everything = jax.tree.map(lambda part: lax.all_gather(part, axis), shard)]
    pallas_call x0 -> x1, Pallas kernels: none -> 25.2 us  [shards(): pl.pallas_call(functools.partial(kernel, n, nh, heads, pieces, rows_f, ro...]
    add x30 -> x0, other arithmetic: 15.2 us -> none  [the longest x15 11.3 us: join_parts(): total = first[1] * scale_one + second[1] * scale_two]
    dynamic_slice x15 -> x0, local copies, waits for them, and re-layouts: 13.9 us -> none  [step(): return combine(so_far, jax.tree.map(lambda part: part[k], everything))]
    dot_general x9 -> x0, matrix products: 13.3 us -> none  [the longest x1 4.24 us: shards(): jnp.einsum('sqhe,skhe->shqk', query_rows, cache_kv[..., :DH], preferred_e...]
    slice x4 -> x0, local copies, waits for them, and re-layouts: 9.01 us -> none  [the longest x1 8.08 us: shards(): cache_kv[..., DH:]]
    while x7 -> x0, local copies, waits for them, and re-layouts: 4.8 us -> none  [merged(): return lax.fori_loop(1, lax.axis_size(axis), step, leading)]
    reduce_scatter x1 -> x0, waiting for transfers between devices: 3.45 us -> none  [shards(): lax.psum_scatter(partial_out, 'head', scatter_dimension=1, tiled=True)]
  transfers between devices with their start and end apart: 2 -> 0, of which waited for: 1 -> 0; matrix products, arithmetic and copies ran while one was open for 3% -> 0% of each run, Pallas kernels for 0% -> 0%
where the time goes in v1:
time: 30.7 us; the launch traced here: 30.3 us
  Pallas kernels  25.2 us (82%)
  local copies, waits for them, and re-layouts  2.76 us (9%)
  matrix products  1.27 us (4%)
  other arithmetic  1 us (3%)
    pallas_call x1, Pallas kernels, shards(): pl.pallas_call(functools.partial(kernel, n, nh, heads, pieces, rows_f, ro...  25.2 us
    unnamed x13, local copies, waits for them, and re-layouts  2.72 us
    dot_general x1, matrix products, shards(): proj = jnp.einsum('td,dhe->the', normed, w_qkv, preferred_element_type=f32)  1.27 us
    reduce_sum x1, other arithmetic, shards(): jnp.mean(xf * xf, axis=-1, keepdims=True) + norm_eps  0.99 us

profile of v1, /device:TPU:0, one launch (start us, length us, event | category | flops | bytes accessed | tf_op | source)
XLA Modules:
  0.0 30.3 jit_solution(5805543329496328407)
XLA Ops:
  0.0 0.0 copy-start
  0.0 0.0 copy-start.5
  0.0 0.0 copy-start.4
  0.0 0.0 copy-start.2
  0.0 0.0 copy-start.3
  0.0 1.0 %fusion.8 = f32[5]{0:T(128)S(1)} fusion(bf16[5,1024]{1,0:T(8,128)(2,1)} %param.9), kind=kLoop, calls=%fused_computation.6 | loop fusion | flops 15355 | bytes 10260 | tf_op jit(solution)/shard_map/reduce_sum | solution.py:258
  1.0 0.9 %copy-done = bf16[1024,4,384]{2,1,0:T(4,128)(2,1)S(1)} copy-done((bf16[1024,4,384]{2,1,0:T(4,128)(2,1)S(1)}, bf16[1024,4,384]{2,1,0:T(4,128)(2,1)}, u32[]{:S(2)}) %copy-start) | copy-done | bytes 3145752
  1.9 1.3 %fusion.5 = bf16[5,4,384]{2,0,1:T(8,128)(2,1)S(1)} fusion(bf16[1024,4,384]{2,1,0:T(4,128)(2,1)S(1)} %copy-done, f32[384]{0:T(512)S(1)} %fusion.15, bf16[5,1024]{1,0:T(8,128)(2,1)} %param.9, f32[1024]{0:T(1024)} %param.10, f32[5]{0:T(128)S(1)} %add_rsqrt_fusion), kind=kOutput, calls=%fused_computation.3 | convolution fusion | flops 15764480 | bytes 3176980 | tf_op jit(solution)/shard_map/td,dhe->the/dot_general | solution.py:260
  3.2 0.0 copy-done.5
  3.2 0.0 copy-done.4
  3.3 0.0 copy-done.2
  3.3 0.0 copy-done.3
  3.3 0.0 copy-start.1
  3.3 1.2 %copy-done.1 = bf16[4,128,1024]{2,1,0:T(8,128)(2,1)S(1)} copy-done((bf16[4,128,1024]{2,1,0:T(8,128)(2,1)S(1)}, bf16[4,128,1024]{2,1,0:T(8,128)(2,1)}, u32[]{:S(2)}) %copy-start.1) | copy-done | bytes 1048600
  4.5 25.2 %shard_map.91 = bf16[5,512]{1,0:T(8,128)(2,1)S(1)} custom-call(bf16[32,384]{1,0:T(8,128)(2,1)S(1)} %pad.4.qkv_ref, bf16[64,256]{1,0:T(8,128)(2,1)S(1)} %bitcast.9, s32[8]{0:T(128)S(1)} %copy-done.4, s32[8]{0:T(128)S(1)} %copy-done.5, bf16[8,512,2,4,128]{4,3,2,1,0:T(4,128)(2,1)} %bitcast.10, bf16[4,128,128]{2,1,0:T(8,128)(2,1)S(1)} %bitcast.8, ...), custom_call_target="tpu_custom_call" | custom-call | flops 100000000 | bytes 10000000 | tf_op jit(solution)/shard_map/pallas_call | solution.py:274
  29.7 0.6 %copy.19 = bf16[5,512]{1,0:T(8,128)(2,1)} copy(bf16[5,512]{1,0:T(8,128)(2,1)S(1)} %shard_map.91) | data formatting | bytes 10240
  (5 shorter events, 0.1 us)
Async XLA Ops:
  0.0 1.9 %copy-start = (bf16[1024,4,384]{2,1,0:T(4,128)(2,1)S(1)}, bf16[1024,4,384]{2,1,0:T(4,128)(2,1)}, u32[]{:S(2)}) copy-start(bf16[1024,4,384]{2,1,0:T(4,128)(2,1)} %param.11) | copy-start | bytes 9437188
  0.0 3.2 %copy-start.5 = (s32[8]{0:T(128)S(1)}, s32[8]{0:T(128)}, u32[]{:S(2)}) copy-start(s32[8]{0:T(128)} %len_ref.1) | copy-start | bytes 100
  0.0 3.2 %copy-start.4 = (s32[8]{0:T(128)S(1)}, s32[8]{0:T(128)}, u32[]{:S(2)}) copy-start(s32[8]{0:T(128)} %owner_ref.1) | copy-start | bytes 100
  0.0 3.2 %copy-start.2 = (bf16[1,4,128,128]{3,2,1,0:T(8,128)(2,1)S(1)}, bf16[1,4,128,128]{3,2,1,0:T(8,128)(2,1)}, u32[]{:S(2)}) copy-start(bf16[1,4,128,128]{3,2,1,0:T(8,128)(2,1)} %param.13) | copy-start | bytes 393220
  0.0 3.3 %copy-start.3 = (bf16[4,16,256]{2,1,0:T(8,128)(2,1)S(1)}, bf16[4,16,256]{2,1,0:T(8,128)(2,1)}, u32[]{:S(2)}) copy-start(bf16[4,16,256]{2,1,0:T(8,128)(2,1)} %param.12) | copy-start | bytes 98308
  3.3 1.2 %copy-start.1 = (bf16[4,128,1024]{2,1,0:T(8,128)(2,1)S(1)}, bf16[4,128,1024]{2,1,0:T(8,128)(2,1)}, u32[]{:S(2)}) copy-start(bf16[4,128,1024]{2,1,0:T(8,128)(2,1)} %w_out_ref.1) | copy-start | bytes 3145732

commit v2 on v1

--- a/solution.py
+++ b/solution.py
@@ -38,10 +38,11 @@
 
 def kernel(
     n, nh, heads, pieces, rows_f, rows,
-    qkv_ref, persist_ref, owner_ref, len_ref, cache_ref, memory_ref, w_out_ref,
+    owner_ref, len_ref, tokens_ref, gain_ref, w_qkv_ref, persist_ref, cache_ref, memory_ref, w_out_ref,
     out_ref,
-    keys, values, memory, w_out, all_query, outbox, inbox, partial, halves,
-    key_sem, value_sem, weight_sem, q_send, q_recv, p_send, p_recv, h_send, h_recv,
+    tokens, gain, w_qkv, persist, keys, values, memory, w_out,
+    all_query, made, outbox, inbox, partial, halves,
+    key_sem, value_sem, weight_sem, w_qkv_sem, q_send, q_recv, p_send, p_recv, h_send, h_recv,
 ):
     me = lax.axis_index("req")
     my_head = lax.axis_index("head")
@@ -58,25 +59,63 @@
             pltpu.make_async_copy(value_view, values.at[s], value_sem.at[s]),
         )
 
-    memory_copy = pltpu.make_async_copy(memory_ref, memory, weight_sem.at[0])
-    w_out_copy = pltpu.make_async_copy(w_out_ref, w_out, weight_sem.at[1])
+    def w_qkv_copy(c):
+        view = w_qkv_ref.at[:, c] if heads > 1 else w_qkv_ref.at[:, pl.ds(c * DH, DH)]
+        return pltpu.make_async_copy(view, w_qkv.at[c], w_qkv_sem.at[c])
+
+    tokens_copy = pltpu.make_async_copy(tokens_ref, tokens, weight_sem.at[0])
+    gain_copy = pltpu.make_async_copy(gain_ref, gain, weight_sem.at[1])
+    persist_copy = pltpu.make_async_copy(persist_ref, persist, weight_sem.at[2])
+    memory_copy = pltpu.make_async_copy(memory_ref, memory, weight_sem.at[3])
+    w_out_copy = pltpu.make_async_copy(w_out_ref, w_out, weight_sem.at[4])
+    tokens_copy.start()
+    gain_copy.start()
+    for c in range(3):
+        w_qkv_copy(c).start()
+
+    barrier = pltpu.get_barrier_semaphore()
+
+    @pl.loop(1, n)
+    def _(k):
+        pl.semaphore_signal(barrier, inc=1, device_id={"req": lax.rem(me + k, n)}, device_id_type=MESH)
+
+    @pl.loop(1, nh)
+    def _(k):
+        pl.semaphore_signal(barrier, inc=1, device_id={"head": lax.rem(my_head + k, nh)}, device_id_type=MESH)
+
+    persist_copy.start()
     memory_copy.start()
     for s in range(pieces):
         for copy in cache_copies(s):
             copy.start()
     w_out_copy.start()
 
-    barrier = pltpu.get_barrier_semaphore()
-
-    @pl.loop(1, n)
-    def _(k):
-        pl.semaphore_signal(barrier, inc=1, device_id={"req": lax.rem(me + k, n)}, device_id_type=MESH)
-
-    @pl.loop(1, nh)
-    def _(k):
-        pl.semaphore_signal(barrier, inc=1, device_id={"head": lax.rem(my_head + k, nh)}, device_id_type=MESH)
-
-    all_query[me] = qkv_ref[:, :DH]
+    tokens_copy.wait()
+    gain_copy.wait()
+    x = tokens[...].astype(f32)
+    width = x.shape[1]
+    normed = (x * lax.rsqrt(jnp.mean(x * x, axis=-1, keepdims=True) + norm_eps) * gain[...]).astype(bf16)
+    spread = (iota((rows_f, Q), 0) // heads == iota((rows_f, Q), 1)).astype(f32).astype(bf16)
+    repeated = dot(spread, normed)
+    if heads > 1:
+        blocks = width // DH
+        stacked = jnp.concatenate([repeated[:, b * DH : (b + 1) * DH] for b in range(blocks)], axis=0)
+        widen = (iota((DH, DH * heads), 0) == iota((DH, DH * heads), 1) // heads).astype(f32).astype(bf16)
+        wide = dot(stacked.astype(bf16), widen)
+        same = iota((rows_f, DH * heads), 0) % heads == iota((rows_f, DH * heads), 1) % heads
+        repeated = jnp.concatenate(
+            [jnp.where(same, wide[b * rows_f : (b + 1) * rows_f], 0.0) for b in range(blocks)], axis=1
+        )
+    repeated = repeated.astype(bf16)
+    w_rows = w_qkv.reshape(3, width * heads, DH)
+
+    def project(c, scale):
+        w_qkv_copy(c).wait()
+        part = dot(repeated, w_rows[c]) * scale
+        return jnp.concatenate([part, jnp.zeros((rows - rows_f, DH), f32)], axis=0).astype(bf16)
+
+    query = project(0, DH ** (-0.5))
+    all_query[me] = query
     pl.semaphore_wait(barrier, n - 1 + nh - 1)
 
     def query_copy(slot, other):
@@ -90,27 +129,32 @@
     def _(k):
         query_copy(me, lax.rem(me + k, n)).start()
 
-    query = qkv_ref[:, :DH]
+    new_key = project(1, 1.0)
+    new_value = project(2, 1.0)
     query_f = query[:rows_f]
-    persist = persist_ref[...]
+    persist_copy.wait()
     row = iota((rows_f, 1), 0)
     row_head, row_token = row % heads, row // heads
     col = iota((1, heads * NP), 1)
     score_persist = jnp.where(row_head == col // NP, dot_t(query_f, persist[:, :DH]), masked_score)
     col = iota((1, rows), 1)
     seen = (row_head == col % heads) & (col // heads <= row_token) & (col < Q * heads)
-    score_new = jnp.where(seen, dot_t(query_f, qkv_ref[:, DH : 2 * DH]), masked_score)
+    score_new = jnp.where(seen, dot_t(query_f, new_key), masked_score)
     m_own = jnp.maximum(
         jnp.max(score_persist, axis=-1, keepdims=True), jnp.max(score_new, axis=-1, keepdims=True)
     )
     w_persist = jnp.exp(score_persist - m_own)
     w_new = jnp.exp(score_new - m_own)
     l_own = jnp.sum(w_persist, axis=-1, keepdims=True) + jnp.sum(w_new, axis=-1, keepdims=True)
-    o_own = dot(w_persist.astype(bf16), persist[:, DH:]) + dot(w_new.astype(bf16), qkv_ref[:, 2 * DH :])
+    o_own = dot(w_persist.astype(bf16), persist[:, DH:]) + dot(w_new.astype(bf16), new_value)
     memory_copy.wait()
     recalled = jnp.zeros((rows_f, DH), f32)
     for h in range(heads):
         recalled = jnp.where(row_head == h, dot(query_f, memory[h]), recalled)
+
+    for s in range(pieces):
+        for copy in cache_copies(s):
+            copy.wait()
 
     @pl.loop(1, n)
     def _(k):
@@ -124,47 +168,53 @@
     owners, peaks, totals, sums = [], [], [], []
     for s in range(pieces):
         owner = owner_ref[s]
-        key_copy, value_copy = cache_copies(s)
-        key_copy.wait()
         valid = same_head & (col_slot < len_ref[s])
         scores = jnp.where(valid, dot_t(all_query[owner][:rows_f], key_rows[s]), masked_score)
         peak = jnp.max(scores, axis=-1, keepdims=True)
         weight = jnp.where(valid, jnp.exp(scores - peak), 0.0)
-        value_copy.wait()
         owners.append(owner)
         peaks.append(peak)
         totals.append(jnp.sum(weight, axis=-1, keepdims=True))
         sums.append(dot(weight.astype(bf16), value_rows[s]))
 
-    shared = []
-    for s in range(pieces):
-        peak = peaks[s]
-        for other in range(pieces):
-            if other != s:
-                peak = jnp.maximum(peak, jnp.where(owners[other] == owners[s], peaks[other], masked_score))
-        shared.append(peak)
-    for s in range(pieces):
-        factor = jnp.exp(peaks[s] - shared[s])
-        totals[s] = totals[s] * factor
-        sums[s] = sums[s] * factor
-
     eye = iota((rows_f, DH), 0) == iota((rows_f, DH), 1)
     zeros_tail = jnp.zeros((2, DH), f32)
 
     def as_row(column):
         return jnp.sum(jnp.where(eye, column, 0.0), axis=0, keepdims=True)
 
+    def send_form(m, l, o):
+        return jnp.concatenate([o] + three_terms(m) + three_terms(l) + [zeros_tail], axis=0).astype(bf16)
+
+    same_owner = [[owners[s] == owners[k] for k in range(pieces)] for s in range(pieces)]
+    shared = []
+    for s in range(pieces):
+        peak = peaks[s]
+        for k in range(pieces):
+            if k != s:
+                peak = jnp.maximum(peak, jnp.where(same_owner[s][k], peaks[k], masked_score))
+        shared.append(peak)
+    peak_rows = [as_row(peak) for peak in shared]
+    total_rows = []
+    for s in range(pieces):
+        factor = jnp.exp(peaks[s] - shared[s])
+        total_rows.append(as_row(totals[s] * factor))
+        sums[s] = sums[s] * factor
+    for s in range(pieces):
+        total, summed = total_rows[s], sums[s]
+        for k in range(pieces):
+            if k != s:
+                total = total + jnp.where(same_owner[s][k], total_rows[k], 0.0)
+                summed = summed + jnp.where(same_owner[s][k], sums[k], 0.0)
+        made[s] = send_form(peak_rows[s], total, summed)
+    nothing = jnp.zeros((1, DH), f32)
+    made[pieces] = send_form(nothing + masked_score, nothing, jnp.zeros((rows_f, DH), f32))
+
     def message(r):
-        m = jnp.full((rows_f, 1), masked_score, f32)
-        l = jnp.zeros((rows_f, 1), f32)
-        o = jnp.zeros((rows_f, DH), f32)
+        which = jnp.int32(pieces)
         for s in range(pieces):
-            mine = owners[s] == r
-            m = jnp.where(mine, shared[s], m)
-            l = l + jnp.where(mine, totals[s], 0.0)
-            o = o + jnp.where(mine, sums[s], 0.0)
-        tail = three_terms(as_row(m)) + three_terms(as_row(l)) + [zeros_tail]
-        return jnp.concatenate([o] + tail, axis=0).astype(bf16)
+            which = jnp.where(owners[s] == r, s, which)
+        return made[which]
 
     def partial_copy(mine, other):
         return pltpu.make_async_remote_copy(
@@ -253,49 +303,51 @@
     columns = w_out.shape[2] // nh
     rows_f = -(-(Q * heads - 8) // 16) * 16 + 8
     rows = rows_f + 8
-    xf = tokens.astype(f32)
-    normed = (
-        xf * lax.rsqrt(jnp.mean(xf * xf, axis=-1, keepdims=True) + norm_eps) * norm_gain
-    ).astype(bf16)
-    proj = jnp.einsum("td,dhe->the", normed, w_qkv, preferred_element_type=f32)
-    scale = jnp.where(jnp.arange(3 * DH) < DH, DH ** (-0.5), 1.0)
-    qkv = (proj * scale).astype(bf16).reshape(Q * heads, 3 * DH)
-    qkv = jnp.pad(qkv, ((0, rows - Q * heads), (0, 0)))
+    width = tokens.shape[1]
     if heads > 1:
         cache = cache_kv.reshape(pieces, slots, heads, 2, DH).transpose(0, 1, 3, 2, 4)
         cache_shape = (pieces, slots, heads, DH)
+        w_qkv = w_qkv.reshape(width, heads, 3, DH).transpose(0, 2, 1, 3)
+        w_shape = (3, width, heads, DH)
     else:
         cache = cache_kv.reshape(pieces, slots, 2 * DH)
         cache_shape = (pieces, slots, DH)
+        w_qkv = w_qkv.reshape(width, 3 * DH)
+        w_shape = (3, width, DH)
     vmem = pl.BlockSpec(memory_space=pltpu.VMEM)
     smem = pl.BlockSpec(memory_space=pltpu.SMEM)
-    hbm = pl.BlockSpec(memory_space=pl.ANY)
+    hbm = pl.BlockSpec(memory_space=pltpu.HBM)
     dma = pltpu.SemaphoreType.DMA
     return pl.pallas_call(
         functools.partial(kernel, n, nh, heads, pieces, rows_f, rows),
         out_shape=jax.ShapeDtypeStruct((Q, columns), bf16),
-        in_specs=[vmem, vmem, smem, smem, hbm, hbm, hbm],
+        in_specs=[smem, smem] + [hbm] * 7,
         out_specs=vmem,
         scratch_shapes=[
+            pltpu.VMEM((Q, width), bf16),
+            pltpu.VMEM((1, width), f32),
+            pltpu.VMEM(w_shape, bf16),
+            pltpu.VMEM((heads * NP, 2 * DH), bf16),
             pltpu.VMEM(cache_shape, bf16),
             pltpu.VMEM(cache_shape, bf16),
             pltpu.VMEM((heads, DH, DH), bf16),
             pltpu.VMEM((heads, DH, nh * columns), bf16),
             pltpu.VMEM((n, rows, DH), bf16),
+            pltpu.VMEM((pieces + 1, rows, DH), bf16),
             pltpu.VMEM((n, rows, DH), bf16),
             pltpu.VMEM((n, rows, DH), bf16),
             pltpu.VMEM((nh, 8, columns), f32),
             pltpu.VMEM((nh, 8, columns), f32),
-            dma((pieces,)), dma((pieces,)), dma((2,)),
+            dma((pieces,)), dma((pieces,)), dma((5,)), dma((3,)),
             dma((n,)), dma((n,)), dma((n,)), dma((n,)), dma((nh,)), dma((nh,)),
         ],
         compiler_params=pltpu.CompilerParams(
-            collective_id=0, has_side_effects=True, vmem_limit_bytes=48 * 2**20
+            collective_id=0, has_side_effects=True, vmem_limit_bytes=64 * 2**20 - 16384
         ),
         cost_estimate=pl.CostEstimate(flops=100_000_000, bytes_accessed=10_000_000, transcendentals=500_000),
     )(
-        qkv, persist_kv.reshape(heads * NP, 2 * DH), piece_owner, piece_len, cache,
-        memory.reshape(heads, DH, DH), w_out,
+        piece_owner, piece_len, tokens, norm_gain.reshape(1, width), w_qkv,
+        persist_kv.reshape(heads * NP, 2 * DH), cache, memory.reshape(heads, DH, DH), w_out,
     )
 
 

time: 30.7 us -> 26 us (0.85)
  local copies, waits for them, and re-layouts: 2.76 us -> 1.3 us
  matrix products: 1.27 us -> 0 us
  other arithmetic: 1 us -> 0 us
  Pallas kernels: 25.2 us -> 24.5 us
    unnamed x13 -> x1, local copies, waits for them, and re-layouts: 2.72 us -> 1.3 us
    dot_general x1 -> x0, matrix products: 1.27 us -> none  [shards(): proj = jnp.einsum('td,dhe->the', normed, w_qkv, preferred_element_type=f32)]
    reduce_sum x1 -> x0, other arithmetic: 0.99 us -> none  [shards(): jnp.mean(xf * xf, axis=-1, keepdims=True) + norm_eps]
    pallas_call x1, Pallas kernels: 25.2 us -> 24.5 us  [shards(): pl.pallas_call(functools.partial(kernel, n, nh, heads, pieces, rows_f, ro...]
where the time goes in v2:
time: 26 us; the launch traced here: 25.8 us
  Pallas kernels  24.5 us (94%)
  local copies, waits for them, and re-layouts  1.3 us (5%)
    pallas_call x1, Pallas kernels, shards(): pl.pallas_call(functools.partial(kernel, n, nh, heads, pieces, rows_f, ro...  24.5 us
    unnamed x1, local copies, waits for them, and re-layouts  1.3 us

profile of v2, /device:TPU:0, one launch (start us, length us, event | category | flops | bytes accessed | tf_op | source)
XLA Modules:
  0.0 25.8 jit_solution(5849934600406029708)
XLA Ops:
  0.0 24.5 %shard_map.91 = bf16[5,512]{1,0:T(8,128)(2,1)} custom-call(s32[8]{0:T(128)} %owner_ref.1, s32[8]{0:T(128)} %len_ref.1, bf16[5,1024]{1,0:T(8,128)(2,1)} %tokens_ref.1, f32[1,1024]{1,0:T(1,128)} %bitcast.13, bf16[1024,3,4,128]{3,2,1,0:T(4,128)(2,1)} %bitcast.10, bf16[64,256]{1,0:T(8,128)(2,1)} %bitcast.12, bf16[8,512,2,4,128]{4,3,2,1,0:T(4,128)(2,1)} %bitcast.9, ...), custom_call_target="tpu_custom_call" | custom-call | flops 100000000 | bytes 10000000 | tf_op jit(solution)/shard_map/pallas_call | solution.py:321
  24.5 1.3 %copy.11 = bf16[5,512]{1,0:T(8,128)(2,1)} copy(bf16[5,512]{1,0:T(8,128)(2,1)} %shard_map.91) | data formatting | bytes 10240

commit v3 on v2

--- a/solution.py
+++ b/solution.py
@@ -28,6 +28,14 @@
 
 def iota(shape, dim):
     return lax.broadcasted_iota(jnp.int32, shape, dim)
+
+
+def each(count, body):
+    if count <= 16:
+        for k in range(1, count):
+            body(k)
+    else:
+        pl.loop(1, count)(body)
 
 
 def three_terms(x):
@@ -75,11 +83,11 @@
 
     barrier = pltpu.get_barrier_semaphore()
 
-    @pl.loop(1, n)
+    @functools.partial(each, n)
     def _(k):
         pl.semaphore_signal(barrier, inc=1, device_id={"req": lax.rem(me + k, n)}, device_id_type=MESH)
 
-    @pl.loop(1, nh)
+    @functools.partial(each, nh)
     def _(k):
         pl.semaphore_signal(barrier, inc=1, device_id={"head": lax.rem(my_head + k, nh)}, device_id_type=MESH)
 
@@ -111,21 +119,30 @@
 
     def project(c, scale):
         w_qkv_copy(c).wait()
-        part = dot(repeated, w_rows[c]) * scale
+        long = width * heads // 4
+        parts = [dot(repeated[:, k * long : (k + 1) * long], w_rows[c, k * long : (k + 1) * long]) for k in range(4)]
+        part = ((parts[0] + parts[1]) + (parts[2] + parts[3])) * scale
         return jnp.concatenate([part, jnp.zeros((rows - rows_f, DH), f32)], axis=0).astype(bf16)
 
     query = project(0, DH ** (-0.5))
     all_query[me] = query
     pl.semaphore_wait(barrier, n - 1 + nh - 1)
 
+    def all_others(buffer, send_sem, recv_sem):
+        return pltpu.make_async_remote_copy(
+            src_ref=buffer.at[pl.ds(0, n - 1)], dst_ref=buffer.at[pl.ds(0, n - 1)],
+            send_sem=send_sem, recv_sem=recv_sem,
+            device_id={"req": lax.rem(me + 1, n)}, device_id_type=MESH,
+        )
+
     def query_copy(slot, other):
         return pltpu.make_async_remote_copy(
             src_ref=all_query.at[slot], dst_ref=all_query.at[slot],
-            send_sem=q_send.at[other], recv_sem=q_recv.at[slot],
+            send_sem=q_send, recv_sem=q_recv,
             device_id={"req": other}, device_id_type=MESH,
         )
 
-    @pl.loop(1, n)
+    @functools.partial(each, n)
     def _(k):
         query_copy(me, lax.rem(me + k, n)).start()
 
@@ -156,9 +173,8 @@
         for copy in cache_copies(s):
             copy.wait()
 
-    @pl.loop(1, n)
-    def _(k):
-        query_copy(lax.rem(me + k, n), lax.rem(me + k, n)).wait_recv()
+    all_queries = all_others(all_query, q_send, q_recv)
+    all_queries.wait_recv()
 
     col = iota((1, slots * heads), 1)
     same_head = row_head == col % heads
@@ -219,11 +235,11 @@
     def partial_copy(mine, other):
         return pltpu.make_async_remote_copy(
             src_ref=outbox.at[other], dst_ref=inbox.at[mine],
-            send_sem=p_send.at[other], recv_sem=p_recv.at[mine],
+            send_sem=p_send, recv_sem=p_recv,
             device_id={"req": other}, device_id_type=MESH,
         )
 
-    @pl.loop(1, n)
+    @functools.partial(each, n)
     def _(k):
         other = lax.rem(me + k, n)
         outbox[other] = message(other)
@@ -231,10 +247,8 @@
 
     inbox[me] = message(me)
 
-    @pl.loop(1, n)
-    def _(k):
-        other = lax.rem(me + k, n)
-        partial_copy(other, other).wait_recv()
+    all_partials = all_others(inbox, p_send, p_recv)
+    all_partials.wait_recv()
 
     got = inbox[...].astype(f32)
     tail = got[:, rows_f:]
@@ -273,26 +287,23 @@
             device_id={"head": other}, device_id_type=MESH,
         )
 
-    @pl.loop(1, nh)
+    @functools.partial(each, nh)
     def _(k):
         half_copy(my_head, lax.rem(my_head + k, nh)).start()
 
     halves[my_head] = partial[my_head]
 
-    @pl.loop(1, nh)
+    @functools.partial(each, nh)
     def _(k):
         other = lax.rem(my_head + k, nh)
         half_copy(other, other).wait_recv()
 
     out_ref[...] = jnp.sum(halves[...], axis=0)[:Q].astype(bf16)
 
-    @pl.loop(1, n)
-    def _(k):
-        other = lax.rem(me + k, n)
-        query_copy(me, other).wait_send()
-        partial_copy(me, other).wait_send()
-
-    @pl.loop(1, nh)
+    all_queries.wait_send()
+    all_partials.wait_send()
+
+    @functools.partial(each, nh)
     def _(k):
         half_copy(my_head, lax.rem(my_head + k, nh)).wait_send()
 
@@ -320,7 +331,7 @@
     dma = pltpu.SemaphoreType.DMA
     return pl.pallas_call(
         functools.partial(kernel, n, nh, heads, pieces, rows_f, rows),
-        out_shape=jax.ShapeDtypeStruct((Q, columns), bf16),
+        out_shape=pltpu.VMEM((Q, columns), bf16),
         in_specs=[smem, smem] + [hbm] * 7,
         out_specs=vmem,
         scratch_shapes=[
@@ -339,10 +350,10 @@
             pltpu.VMEM((nh, 8, columns), f32),
             pltpu.VMEM((nh, 8, columns), f32),
             dma((pieces,)), dma((pieces,)), dma((5,)), dma((3,)),
-            dma((n,)), dma((n,)), dma((n,)), dma((n,)), dma((nh,)), dma((nh,)),
+            dma, dma, dma, dma, dma((nh,)), dma((nh,)),
         ],
         compiler_params=pltpu.CompilerParams(
-            collective_id=0, has_side_effects=True, vmem_limit_bytes=64 * 2**20 - 16384
+            collective_id=0, has_side_effects=True, vmem_limit_bytes=62 * 2**20
         ),
         cost_estimate=pl.CostEstimate(flops=100_000_000, bytes_accessed=10_000_000, transcendentals=500_000),
     )(

time: 26 us -> 24.1 us (0.927)
  Pallas kernels: 24.5 us -> 23.3 us
  local copies, waits for them, and re-layouts: 1.3 us -> 0.6 us
    pallas_call x1, Pallas kernels: 24.5 us -> 23.3 us  [shards(): pl.pallas_call(functools.partial(kernel, n, nh, heads, pieces, rows_f, ro...]
    unnamed x1, local copies, waits for them, and re-layouts: 1.3 us -> 0.6 us
where the time goes in v3:
time: 24.1 us; the launch traced here: 23.9 us
  Pallas kernels  23.3 us (97%)
  local copies, waits for them, and re-layouts  0.6 us (2%)
    pallas_call x1, Pallas kernels, shards(): pl.pallas_call(functools.partial(kernel, n, nh, heads, pieces, rows_f, ro...  23.3 us
    unnamed x1, local copies, waits for them, and re-layouts  0.6 us

profile of v3, /device:TPU:0, one launch (start us, length us, event | category | flops | bytes accessed | tf_op | source)
XLA Modules:
  0.0 23.9 jit_solution(11578360097770259712)
XLA Ops:
  0.0 23.3 %shard_map.91 = bf16[5,512]{1,0:T(8,128)(2,1)S(1)} custom-call(s32[8]{0:T(128)} %owner_ref.1, s32[8]{0:T(128)} %len_ref.1, bf16[5,1024]{1,0:T(8,128)(2,1)} %tokens_ref.1, f32[1,1024]{1,0:T(1,128)} %bitcast.13, bf16[1024,3,4,128]{3,2,1,0:T(4,128)(2,1)} %bitcast.10, bf16[64,256]{1,0:T(8,128)(2,1)} %bitcast.12, bf16[8,512,2,4,128]{4,3,2,1,0:T(4,128)(2,1)} %bitcast.9, ...), custom_call_target="tpu_custom_call" | custom-call | flops 100000000 | bytes 10000000 | tf_op jit(solution)/shard_map/pallas_call | solution.py:332
  23.3 0.6 %copy.11 = bf16[5,512]{1,0:T(8,128)(2,1)} copy(bf16[5,512]{1,0:T(8,128)(2,1)S(1)} %shard_map.91) | data formatting | bytes 10240

commit v4 on v3

--- a/solution.py
+++ b/solution.py
@@ -146,14 +146,108 @@
     def _(k):
         query_copy(me, lax.rem(me + k, n)).start()
 
+    query_f = query[:rows_f]
+    row = iota((rows_f, 1), 0)
+    row_head, row_token = row % heads, row // heads
+    memory_copy.wait()
+    recalled = jnp.zeros((rows_f, DH), f32)
+    for h in range(heads):
+        recalled = jnp.where(row_head == h, dot(query_f, memory[h]), recalled)
+    persist_copy.wait()
+    col = iota((1, heads * NP), 1)
+    score_persist = jnp.where(row_head == col // NP, dot_t(query_f, persist[:, :DH]), masked_score)
+
+    for s in range(pieces):
+        for copy in cache_copies(s):
+            copy.wait()
+
+    all_queries = all_others(all_query, q_send, q_recv)
+    all_queries.wait_recv()
+
+    col = iota((1, slots * heads), 1)
+    same_head = row_head == col % heads
+    col_slot = col // heads
+    key_rows = keys.reshape(pieces, slots * heads, DH)
+    value_rows = values.reshape(pieces, slots * heads, DH)
+    owners = [owner_ref[s] for s in range(pieces)]
+    peaks, totals, sums = [], [], []
+    gap = jnp.zeros((rows_f, DH), f32)
+    for s in range(0, pieces, 2):
+        pair = (s, s + 1)
+        first, second = [all_query[owners[k]].astype(f32)[:rows_f] for k in pair]
+        left = jnp.concatenate([first, gap], axis=0)
+        right = jnp.concatenate([gap, second], axis=0)
+        both = jnp.concatenate([left, right], axis=1).astype(bf16)
+        scores = dot_t(both, jnp.concatenate([key_rows[k] for k in pair], axis=1))
+        weights = []
+        for k in pair:
+            valid = same_head & (col_slot < len_ref[k])
+            own_scores = jnp.where(valid, scores[(k - s) * rows_f : (k - s + 1) * rows_f], masked_score)
+            peak = jnp.max(own_scores, axis=-1, keepdims=True)
+            weight = jnp.where(valid, jnp.exp(own_scores - peak), 0.0)
+            peaks.append(peak)
+            totals.append(jnp.sum(weight, axis=-1, keepdims=True))
+            weights.append(weight)
+        weights = jnp.concatenate(weights, axis=0).astype(bf16)
+        summed = dot(weights, jnp.concatenate([value_rows[k] for k in pair], axis=1))
+        sums += [summed[:rows_f, :DH], summed[rows_f:, DH:]]
+
+    eye = iota((rows_f, DH), 0) == iota((rows_f, DH), 1)
+    zeros_tail = jnp.zeros((2, DH), f32)
+
+    def as_row(column):
+        return jnp.sum(jnp.where(eye, column, 0.0), axis=0, keepdims=True)
+
+    def send_form(m, l, o):
+        return jnp.concatenate([o] + three_terms(m) + three_terms(l) + [zeros_tail], axis=0).astype(bf16)
+
+    same_owner = [[owners[s] == owners[k] for k in range(pieces)] for s in range(pieces)]
+    shared = []
+    for s in range(pieces):
+        peak = peaks[s]
+        for k in range(pieces):
+            if k != s:
+                peak = jnp.maximum(peak, jnp.where(same_owner[s][k], peaks[k], masked_score))
+        shared.append(peak)
+    peak_rows = [as_row(peak) for peak in shared]
+    total_rows = []
+    for s in range(pieces):
+        factor = jnp.exp(peaks[s] - shared[s])
+        total_rows.append(as_row(totals[s] * factor))
+        sums[s] = sums[s] * factor
+    for s in range(pieces):
+        total, summed = total_rows[s], sums[s]
+        for k in range(pieces):
+            if k != s:
+                total = total + jnp.where(same_owner[s][k], total_rows[k], 0.0)
+                summed = summed + jnp.where(same_owner[s][k], sums[k], 0.0)
+        made[s] = send_form(peak_rows[s], total, summed)
+    nothing = jnp.zeros((1, DH), f32)
+    made[pieces] = send_form(nothing + masked_score, nothing, jnp.zeros((rows_f, DH), f32))
+
+    def message(r):
+        which = jnp.int32(pieces)
+        for s in range(pieces):
+            which = jnp.where(owners[s] == r, s, which)
+        return made[which]
+
+    def partial_copy(mine, other):
+        return pltpu.make_async_remote_copy(
+            src_ref=outbox.at[other], dst_ref=inbox.at[mine],
+            send_sem=p_send, recv_sem=p_recv,
+            device_id={"req": other}, device_id_type=MESH,
+        )
+
+    @functools.partial(each, n)
+    def _(k):
+        other = lax.rem(me + k, n)
+        outbox[other] = message(other)
+        partial_copy(me, other).start()
+
+    inbox[me] = message(me)
+
     new_key = project(1, 1.0)
     new_value = project(2, 1.0)
-    query_f = query[:rows_f]
-    persist_copy.wait()
-    row = iota((rows_f, 1), 0)
-    row_head, row_token = row % heads, row // heads
-    col = iota((1, heads * NP), 1)
-    score_persist = jnp.where(row_head == col // NP, dot_t(query_f, persist[:, :DH]), masked_score)
     col = iota((1, rows), 1)
     seen = (row_head == col % heads) & (col // heads <= row_token) & (col < Q * heads)
     score_new = jnp.where(seen, dot_t(query_f, new_key), masked_score)
@@ -164,88 +258,6 @@
     w_new = jnp.exp(score_new - m_own)
     l_own = jnp.sum(w_persist, axis=-1, keepdims=True) + jnp.sum(w_new, axis=-1, keepdims=True)
     o_own = dot(w_persist.astype(bf16), persist[:, DH:]) + dot(w_new.astype(bf16), new_value)
-    memory_copy.wait()
-    recalled = jnp.zeros((rows_f, DH), f32)
-    for h in range(heads):
-        recalled = jnp.where(row_head == h, dot(query_f, memory[h]), recalled)
-
-    for s in range(pieces):
-        for copy in cache_copies(s):
-            copy.wait()
-
-    all_queries = all_others(all_query, q_send, q_recv)
-    all_queries.wait_recv()
-
-    col = iota((1, slots * heads), 1)
-    same_head = row_head == col % heads
-    col_slot = col // heads
-    key_rows = keys.reshape(pieces, slots * heads, DH)
-    value_rows = values.reshape(pieces, slots * heads, DH)
-    owners, peaks, totals, sums = [], [], [], []
-    for s in range(pieces):
-        owner = owner_ref[s]
-        valid = same_head & (col_slot < len_ref[s])
-        scores = jnp.where(valid, dot_t(all_query[owner][:rows_f], key_rows[s]), masked_score)
-        peak = jnp.max(scores, axis=-1, keepdims=True)
-        weight = jnp.where(valid, jnp.exp(scores - peak), 0.0)
-        owners.append(owner)
-        peaks.append(peak)
-        totals.append(jnp.sum(weight, axis=-1, keepdims=True))
-        sums.append(dot(weight.astype(bf16), value_rows[s]))
-
-    eye = iota((rows_f, DH), 0) == iota((rows_f, DH), 1)
-    zeros_tail = jnp.zeros((2, DH), f32)
-
-    def as_row(column):
-        return jnp.sum(jnp.where(eye, column, 0.0), axis=0, keepdims=True)
-
-    def send_form(m, l, o):
-        return jnp.concatenate([o] + three_terms(m) + three_terms(l) + [zeros_tail], axis=0).astype(bf16)
-
-    same_owner = [[owners[s] == owners[k] for k in range(pieces)] for s in range(pieces)]
-    shared = []
-    for s in range(pieces):
-        peak = peaks[s]
-        for k in range(pieces):
-            if k != s:
-                peak = jnp.maximum(peak, jnp.where(same_owner[s][k], peaks[k], masked_score))
-        shared.append(peak)
-    peak_rows = [as_row(peak) for peak in shared]
-    total_rows = []
-    for s in range(pieces):
-        factor = jnp.exp(peaks[s] - shared[s])
-        total_rows.append(as_row(totals[s] * factor))
-        sums[s] = sums[s] * factor
-    for s in range(pieces):
-        total, summed = total_rows[s], sums[s]
-        for k in range(pieces):
-            if k != s:
-                total = total + jnp.where(same_owner[s][k], total_rows[k], 0.0)
-                summed = summed + jnp.where(same_owner[s][k], sums[k], 0.0)
-        made[s] = send_form(peak_rows[s], total, summed)
-    nothing = jnp.zeros((1, DH), f32)
-    made[pieces] = send_form(nothing + masked_score, nothing, jnp.zeros((rows_f, DH), f32))
-
-    def message(r):
-        which = jnp.int32(pieces)
-        for s in range(pieces):
-            which = jnp.where(owners[s] == r, s, which)
-        return made[which]
-
-    def partial_copy(mine, other):
-        return pltpu.make_async_remote_copy(
-            src_ref=outbox.at[other], dst_ref=inbox.at[mine],
-            send_sem=p_send, recv_sem=p_recv,
-            device_id={"req": other}, device_id_type=MESH,
-        )
-
-    @functools.partial(each, n)
-    def _(k):
-        other = lax.rem(me + k, n)
-        outbox[other] = message(other)
-        partial_copy(me, other).start()
-
-    inbox[me] = message(me)
 
     all_partials = all_others(inbox, p_send, p_recv)
     all_partials.wait_recv()
@@ -276,10 +288,6 @@
     by_head = dot(pick.astype(f32).astype(bf16), head_out)
     lanes = jnp.concatenate([by_head[8 * h : 8 * h + 8] for h in range(heads)], axis=1).astype(bf16)
     w_out_copy.wait()
-    layer = dot(lanes, w_out[...].reshape(heads * DH, nh * columns))
-    for k in range(nh):
-        partial[k] = layer[:, k * columns : (k + 1) * columns]
-
     def half_copy(mine, other):
         return pltpu.make_async_remote_copy(
             src_ref=partial.at[other], dst_ref=halves.at[mine],
@@ -287,11 +295,17 @@
             device_id={"head": other}, device_id_type=MESH,
         )
 
+    def layer_part(k):
+        start = pl.multiple_of(k * columns, columns)
+        return dot(lanes, w_out[:, :, pl.ds(start, columns)].reshape(heads * DH, columns))
+
     @functools.partial(each, nh)
     def _(k):
-        half_copy(my_head, lax.rem(my_head + k, nh)).start()
-
-    halves[my_head] = partial[my_head]
+        other = lax.rem(my_head + k, nh)
+        partial[other] = layer_part(other)
+        half_copy(my_head, other).start()
+
+    halves[my_head] = layer_part(my_head)
 
     @functools.partial(each, nh)
     def _(k):

time: 24.1 us -> 23 us (0.954)
  Pallas kernels: 23.3 us -> 22.3 us
    pallas_call x1, Pallas kernels: 23.3 us -> 22.3 us  [shards(): pl.pallas_call(functools.partial(kernel, n, nh, heads, pieces, rows_f, ro...]
where the time goes in v4:
time: 23 us; the launch traced here: 22.9 us
  Pallas kernels  22.3 us (97%)
  local copies, waits for them, and re-layouts  0.6 us (3%)
    pallas_call x1, Pallas kernels, shards(): pl.pallas_call(functools.partial(kernel, n, nh, heads, pieces, rows_f, ro...  22.3 us
    unnamed x1, local copies, waits for them, and re-layouts  0.6 us

profile of v4, /device:TPU:0, one launch (start us, length us, event | category | flops | bytes accessed | tf_op | source)
XLA Modules:
  0.0 22.9 jit_solution(6663308746851210776)
XLA Ops:
  0.0 22.3 %shard_map.91 = bf16[5,512]{1,0:T(8,128)(2,1)S(1)} custom-call(s32[8]{0:T(128)} %owner_ref.1, s32[8]{0:T(128)} %len_ref.1, bf16[5,1024]{1,0:T(8,128)(2,1)} %tokens_ref.1, f32[1,1024]{1,0:T(1,128)} %bitcast.13, bf16[1024,3,4,128]{3,2,1,0:T(4,128)(2,1)} %bitcast.10, bf16[64,256]{1,0:T(8,128)(2,1)} %bitcast.12, bf16[8,512,2,4,128]{4,3,2,1,0:T(4,128)(2,1)} %bitcast.9, ...), custom_call_target="tpu_custom_call" | custom-call | flops 100000000 | bytes 10000000 | tf_op jit(solution)/shard_map/pallas_call | solution.py:346
  22.3 0.6 %copy.11 = bf16[5,512]{1,0:T(8,128)(2,1)} copy(bf16[5,512]{1,0:T(8,128)(2,1)S(1)} %shard_map.91) | data formatting | bytes 10240

commit v5 on v4

--- a/solution.py
+++ b/solution.py
@@ -32,7 +32,7 @@
 
 def each(count, body):
     if count <= 16:
-        for k in range(1, count):
+        for k in sorted(range(1, count), key=lambda k: abs(2 * k - count)):
             body(k)
     else:
         pl.loop(1, count)(body)
@@ -46,9 +46,9 @@
 
 def kernel(
     n, nh, heads, pieces, rows_f, rows,
-    owner_ref, len_ref, tokens_ref, gain_ref, w_qkv_ref, persist_ref, cache_ref, memory_ref, w_out_ref,
+    owner_hbm, len_hbm, tokens_ref, gain_ref, w_qkv_ref, persist_ref, cache_ref, memory_ref, w_out_ref,
     out_ref,
-    tokens, gain, w_qkv, persist, keys, values, memory, w_out,
+    owner_ref, len_ref, tokens, gain, w_qkv, persist, keys, values, memory, w_out,
     all_query, made, outbox, inbox, partial, halves,
     key_sem, value_sem, weight_sem, w_qkv_sem, q_send, q_recv, p_send, p_recv, h_send, h_recv,
 ):
@@ -56,6 +56,16 @@
     my_head = lax.axis_index("head")
     columns = partial.shape[-1]
     slots = cache_ref.shape[1]
+
+    barrier = pltpu.get_barrier_semaphore()
+
+    @functools.partial(each, n)
+    def _(k):
+        pl.semaphore_signal(barrier, inc=1, device_id={"req": lax.rem(me + k, n)}, device_id_type=MESH)
+
+    @functools.partial(each, nh)
+    def _(k):
+        pl.semaphore_signal(barrier, inc=1, device_id={"head": lax.rem(my_head + k, nh)}, device_id_type=MESH)
 
     def cache_copies(s):
         if heads > 1:
@@ -81,16 +91,10 @@
     for c in range(3):
         w_qkv_copy(c).start()
 
-    barrier = pltpu.get_barrier_semaphore()
-
-    @functools.partial(each, n)
-    def _(k):
-        pl.semaphore_signal(barrier, inc=1, device_id={"req": lax.rem(me + k, n)}, device_id_type=MESH)
-
-    @functools.partial(each, nh)
-    def _(k):
-        pl.semaphore_signal(barrier, inc=1, device_id={"head": lax.rem(my_head + k, nh)}, device_id_type=MESH)
-
+    owner_copy = pltpu.make_async_copy(owner_hbm, owner_ref, weight_sem.at[5])
+    len_copy = pltpu.make_async_copy(len_hbm, len_ref, weight_sem.at[6])
+    owner_copy.start()
+    len_copy.start()
     persist_copy.start()
     memory_copy.start()
     for s in range(pieces):
@@ -114,17 +118,18 @@
         repeated = jnp.concatenate(
             [jnp.where(same, wide[b * rows_f : (b + 1) * rows_f], 0.0) for b in range(blocks)], axis=1
         )
-    repeated = repeated.astype(bf16)
     w_rows = w_qkv.reshape(3, width * heads, DH)
-
-    def project(c, scale):
-        w_qkv_copy(c).wait()
-        long = width * heads // 4
-        parts = [dot(repeated[:, k * long : (k + 1) * long], w_rows[c, k * long : (k + 1) * long]) for k in range(4)]
-        part = ((parts[0] + parts[1]) + (parts[2] + parts[3])) * scale
+    half = width * heads // 2
+
+    def padded(part):
         return jnp.concatenate([part, jnp.zeros((rows - rows_f, DH), f32)], axis=0).astype(bf16)
 
-    query = project(0, DH ** (-0.5))
+    halved = jnp.concatenate([repeated[:, :half], repeated[:, half:]], axis=0).astype(bf16)
+    w_qkv_copy(0).wait()
+    w_halves = jnp.concatenate([w_rows[0, :half], w_rows[0, half:]], axis=1)
+    cut = half // 2
+    crossed = dot(halved[:, :cut], w_halves[:cut]) + dot(halved[:, cut:], w_halves[cut:])
+    query = padded((crossed[:rows_f, :DH] + crossed[rows_f:, DH:]) * DH ** (-0.5))
     all_query[me] = query
     pl.semaphore_wait(barrier, n - 1 + nh - 1)
 
@@ -169,6 +174,8 @@
     col_slot = col // heads
     key_rows = keys.reshape(pieces, slots * heads, DH)
     value_rows = values.reshape(pieces, slots * heads, DH)
+    owner_copy.wait()
+    len_copy.wait()
     owners = [owner_ref[s] for s in range(pieces)]
     peaks, totals, sums = [], [], []
     gap = jnp.zeros((rows_f, DH), f32)
@@ -246,8 +253,12 @@
 
     inbox[me] = message(me)
 
-    new_key = project(1, 1.0)
-    new_value = project(2, 1.0)
+    w_qkv_copy(1).wait()
+    w_qkv_copy(2).wait()
+    whole = repeated.astype(bf16)
+    w_new = jnp.concatenate([w_rows[1], w_rows[2]], axis=1)
+    new = dot(whole[:, :half], w_new[:half]) + dot(whole[:, half:], w_new[half:])
+    new_key, new_value = padded(new[:, :DH]), padded(new[:, DH:])
     col = iota((1, rows), 1)
     seen = (row_head == col % heads) & (col // heads <= row_token) & (col < Q * heads)
     score_new = jnp.where(seen, dot_t(query_f, new_key), masked_score)
@@ -340,15 +351,16 @@
         w_qkv = w_qkv.reshape(width, 3 * DH)
         w_shape = (3, width, DH)
     vmem = pl.BlockSpec(memory_space=pltpu.VMEM)
-    smem = pl.BlockSpec(memory_space=pltpu.SMEM)
     hbm = pl.BlockSpec(memory_space=pltpu.HBM)
     dma = pltpu.SemaphoreType.DMA
     return pl.pallas_call(
         functools.partial(kernel, n, nh, heads, pieces, rows_f, rows),
         out_shape=pltpu.VMEM((Q, columns), bf16),
-        in_specs=[smem, smem] + [hbm] * 7,
+        in_specs=[hbm] * 9,
         out_specs=vmem,
         scratch_shapes=[
+            pltpu.SMEM((pieces,), jnp.int32),
+            pltpu.SMEM((pieces,), jnp.int32),
             pltpu.VMEM((Q, width), bf16),
             pltpu.VMEM((1, width), f32),
             pltpu.VMEM(w_shape, bf16),
@@ -363,7 +375,7 @@
             pltpu.VMEM((n, rows, DH), bf16),
             pltpu.VMEM((nh, 8, columns), f32),
             pltpu.VMEM((nh, 8, columns), f32),
-            dma((pieces,)), dma((pieces,)), dma((5,)), dma((3,)),
+            dma((pieces,)), dma((pieces,)), dma((7,)), dma((3,)),
             dma, dma, dma, dma, dma((nh,)), dma((nh,)),
         ],
         compiler_params=pltpu.CompilerParams(

time: 23 us -> 23.3 us (1.013)
    pallas_call x1, Pallas kernels: 22.3 us -> 22.5 us  [shards(): pl.pallas_call(functools.partial(kernel, n, nh, heads, pieces, rows_f, ro...]
where the time goes in v5:
time: 23.3 us; the launch traced here: 23.1 us
  Pallas kernels  22.5 us (97%)
  local copies, waits for them, and re-layouts  0.6 us (3%)
    pallas_call x1, Pallas kernels, shards(): pl.pallas_call(functools.partial(kernel, n, nh, heads, pieces, rows_f, ro...  22.5 us
    unnamed x1, local copies, waits for them, and re-layouts  0.6 us

profile of v5, /device:TPU:0, one launch (start us, length us, event | category | flops | bytes accessed | tf_op | source)
XLA Modules:
  0.0 23.1 jit_solution(5976577720674521651)
XLA Ops:
  0.0 22.5 %shard_map.91 = bf16[5,512]{1,0:T(8,128)(2,1)S(1)} custom-call(s32[8]{0:T(128)} %owner_hbm.1, s32[8]{0:T(128)} %len_hbm.1, bf16[5,1024]{1,0:T(8,128)(2,1)} %tokens_ref.1, f32[1,1024]{1,0:T(1,128)} %bitcast.13, bf16[1024,3,4,128]{3,2,1,0:T(4,128)(2,1)} %bitcast.10, bf16[64,256]{1,0:T(8,128)(2,1)} %bitcast.12, bf16[8,512,2,4,128]{4,3,2,1,0:T(4,128)(2,1)} %bitcast.9, ...), custom_call_target="tpu_custom_call" | custom-call | flops 100000000 | bytes 10000000 | tf_op jit(solution)/shard_map/pallas_call | solution.py:356
  22.5 0.6 %copy.11 = bf16[5,512]{1,0:T(8,128)(2,1)} copy(bf16[5,512]{1,0:T(8,128)(2,1)S(1)} %shard_map.91) | data formatting | bytes 10240

commit v6 on v5

--- a/solution.py
+++ b/solution.py
@@ -32,7 +32,7 @@
 
 def each(count, body):
     if count <= 16:
-        for k in sorted(range(1, count), key=lambda k: abs(2 * k - count)):
+        for k in range(1, count):
             body(k)
     else:
         pl.loop(1, count)(body)

time: 23.3 us -> 22.4 us (0.961)
  Pallas kernels: 22.5 us -> 21.7 us
    pallas_call x1, Pallas kernels: 22.5 us -> 21.7 us  [shards(): pl.pallas_call(functools.partial(kernel, n, nh, heads, pieces, rows_f, ro...]
where the time goes in v6:
time: 22.4 us; the launch traced here: 22.3 us
  Pallas kernels  21.7 us (97%)
  local copies, waits for them, and re-layouts  0.6 us (3%)
    pallas_call x1, Pallas kernels, shards(): pl.pallas_call(functools.partial(kernel, n, nh, heads, pieces, rows_f, ro...  21.7 us
    unnamed x1, local copies, waits for them, and re-layouts  0.6 us

profile of v6, /device:TPU:0, one launch (start us, length us, event | category | flops | bytes accessed | tf_op | source)
XLA Modules:
  0.0 22.3 jit_solution(171872567200681751)
XLA Ops:
  0.0 21.7 %shard_map.91 = bf16[5,512]{1,0:T(8,128)(2,1)S(1)} custom-call(s32[8]{0:T(128)} %owner_hbm.1, s32[8]{0:T(128)} %len_hbm.1, bf16[5,1024]{1,0:T(8,128)(2,1)} %tokens_ref.1, f32[1,1024]{1,0:T(1,128)} %bitcast.13, bf16[1024,3,4,128]{3,2,1,0:T(4,128)(2,1)} %bitcast.10, bf16[64,256]{1,0:T(8,128)(2,1)} %bitcast.12, bf16[8,512,2,4,128]{4,3,2,1,0:T(4,128)(2,1)} %bitcast.9, ...), custom_call_target="tpu_custom_call" | custom-call | flops 100000000 | bytes 10000000 | tf_op jit(solution)/shard_map/pallas_call | solution.py:356
  21.7 0.6 %copy.11 = bf16[5,512]{1,0:T(8,128)(2,1)} copy(bf16[5,512]{1,0:T(8,128)(2,1)S(1)} %shard_map.91) | data formatting | bytes 10240
